TPU v7x, 32 devices: a whole 2x2x4 slice. The times are simulated.
32 devices in a mesh: groups: 2 (over y), person: 4 (over x, core), frame: 4 (over z).
Axes of the slice: x: 2, y: 2, z: 4, core: 2. Of those that a mesh axis runs over, the one named last changes fastest.
Arguments:
- tokens: bfloat16 [32, 256, 1024], P(('groups', 'person'), 'frame'), parts along dimension 0, may hold values from -6 to 6
- norm_time: float32 [1024], replicated, may hold values from 0.5 to 1.5
- qkv_time: bfloat16 [1024, 3072], replicated, may hold values from -0.1875 to 0.1875
- qgain_time: float32 [64], replicated, may hold values from 0.5 to 1.5
- kgain_time: float32 [64], replicated, may hold values from 0.5 to 1.5
- out_time: bfloat16 [1024, 1024], replicated, may hold values from -0.1875 to 0.1875
- norm_cross: float32 [1024], replicated, may hold values from 0.5 to 1.5
- qkv_cross: bfloat16 [1024, 3072], P('frame'), may hold values from -0.1875 to 0.1875
- qgain_cross: float32 [64], replicated, may hold values from 0.5 to 1.5
- kgain_cross: float32 [64], replicated, may hold values from 0.5 to 1.5
- out_cross: bfloat16 [1024, 1024], P('frame'), may hold values from -0.1875 to 0.1875
- frame_counts: int32 [32], P('groups'), parts along dimension 0, may hold values from 1 to 256, as said below
- presence: int32 [32], P('groups'), parts along dimension 0, may hold values 0 or 1
Outputs:
- block_out: bfloat16 [32, 256, 1024], P(('groups', 'person'), 'frame'), parts along dimension 0
There are 2 independent parts, one for each index of `groups`. A program takes and returns all parts, laid end to end along the dimension named above; an argument that names none is the same for every part. Nothing has to cross between parts.
Inputs may be any that keep to these rules, and one draw needn't show every extreme that they name: `frame_counts`: some person has all 256 frames valid.
All inputs are finite; a program needn't handle non-finite values.
Results may differ from a plain program's by a relative error of at most 0.019.
Values may be sent and summed in bfloat16 or wider, within the bound.
A program may use at most 128 MiB of HBM per device.

v0:
```python
import math

import jax
import jax.numpy as jnp
from jax import lax
from jax.sharding import PartitionSpec as P

H = 16
HD = 64


def norm_rows(entries, gains):
    return entries * lax.rsqrt(jnp.mean(entries * entries, axis=-1, keepdims=True) + 1e-06) * gains


def project(hidden, weight, qgain, kgain):
    leading = hidden.shape[:-1]
    flat_rows = hidden.reshape(-1, hidden.shape[-1])
    joined = jnp.dot(flat_rows, weight, preferred_element_type=jnp.float32).reshape(
        leading + (3, H, HD)
    )
    queries = (norm_rows(joined[..., 0, :, :], qgain) * (3.0 / math.sqrt(HD))).astype(jnp.bfloat16)
    key_rows = norm_rows(joined[..., 1, :, :], kgain).astype(jnp.bfloat16)
    value_rows = joined[..., 2, :, :].astype(jnp.bfloat16)
    return (queries, key_rows, value_rows)


def on_device(
    tokens,
    norm_time,
    qkv_time,
    qgain_time,
    kgain_time,
    out_time,
    norm_cross,
    qkv_cross,
    qgain_cross,
    kgain_cross,
    out_cross,
    frame_counts,
    presence,
):
    person_rows, frame_rows, width = tokens.shape
    person_base = lax.axis_index("person") * person_rows
    frame_base = lax.axis_index("frame") * frame_rows
    cross_qkv, cross_out = (
        lax.all_gather(qkv_cross, "frame", axis=0, tiled=True),
        lax.all_gather(out_cross, "frame", axis=0, tiled=True),
    )
    local_counts = lax.dynamic_slice_in_dim(frame_counts, person_base, person_rows)
    local_present = lax.dynamic_slice_in_dim(presence, person_base, person_rows)
    frame_index = frame_base + jnp.arange(frame_rows, dtype=jnp.int32)
    live_frames = frame_index[None, :] < local_counts[:, None]
    key_flags_time = live_frames.astype(jnp.int32)
    key_flags_cross = (live_frames & (local_present[:, None] == 1)).astype(jnp.int32)
    stream = tokens.astype(jnp.float32)
    hidden = norm_rows(stream, norm_time).astype(jnp.bfloat16)
    queries, key_rows, value_rows = project(hidden, qkv_time, qgain_time, kgain_time)
    spread_flags = jnp.broadcast_to(
        key_flags_time[:, :, None, None], (person_rows, frame_rows, H, 1)
    )

    def attend_one(member):
        query_one, key_one, value_one, flag_one = member
        scores = jnp.einsum("qhd,khd->hqk", query_one, key_one, preferred_element_type=jnp.float32)
        allowed = (flag_one[:, 0, 0] > 0)[None, None, :]
        weights = jnp.where(allowed, jnp.exp(scores), 0.0).astype(jnp.bfloat16)
        summed = jnp.einsum("hqk,khd->qhd", weights, value_one, preferred_element_type=jnp.float32)
        totals = jnp.transpose(jnp.sum(weights.astype(jnp.float32), axis=-1))
        return (summed / totals[:, :, None]).astype(jnp.bfloat16)

    results = lax.map(
        attend_one,
        (
            lax.all_to_all(queries, "frame", split_axis=2, concat_axis=1, tiled=True),
            lax.all_to_all(key_rows, "frame", split_axis=2, concat_axis=1, tiled=True),
            lax.all_to_all(value_rows, "frame", split_axis=2, concat_axis=1, tiled=True),
            lax.all_to_all(spread_flags, "frame", split_axis=2, concat_axis=1, tiled=True),
        ),
    )
    attended = lax.all_to_all(results, "frame", split_axis=1, concat_axis=2, tiled=True)
    token_count = person_rows * frame_rows
    branch = jnp.dot(
        attended.reshape(token_count, width), out_time, preferred_element_type=jnp.float32
    ).reshape(person_rows, frame_rows, width)
    middle = (stream + branch).astype(jnp.bfloat16)
    middle = lax.optimization_barrier(middle)
    stream = middle.astype(jnp.float32)
    hidden = norm_rows(stream, norm_cross).astype(jnp.bfloat16)
    queries, key_rows, value_rows = project(hidden, cross_qkv, qgain_cross, kgain_cross)
    spread_flags = jnp.broadcast_to(
        key_flags_cross[:, :, None, None], (person_rows, frame_rows, H, 1)
    )
    query_all = lax.all_to_all(queries, "person", split_axis=2, concat_axis=0, tiled=True)
    key_all = lax.all_to_all(key_rows, "person", split_axis=2, concat_axis=0, tiled=True)
    value_all = lax.all_to_all(value_rows, "person", split_axis=2, concat_axis=0, tiled=True)
    flag_all = lax.all_to_all(spread_flags, "person", split_axis=2, concat_axis=0, tiled=True)
    people = query_all.shape[0]
    scores = jnp.einsum("qfhd,kfhd->fhqk", query_all, key_all, preferred_element_type=jnp.float32)
    persons = jnp.arange(people, dtype=jnp.int32)
    self_pair = persons[:, None] == persons[None, :]
    allowed = (jnp.transpose(flag_all[:, :, 0, 0])[:, None, None, :] > 0) | self_pair[None, None]
    weights = jnp.where(allowed, jnp.exp(scores), 0.0).astype(jnp.bfloat16)
    summed = jnp.einsum("fhqk,kfhd->qfhd", weights, value_all, preferred_element_type=jnp.float32)
    totals = jnp.transpose(jnp.sum(weights.astype(jnp.float32), axis=3), (2, 0, 1))
    results = (summed / totals[..., None]).astype(jnp.bfloat16)
    attended = lax.all_to_all(results, "person", split_axis=0, concat_axis=2, tiled=True)
    branch = jnp.dot(
        attended.reshape(token_count, width), cross_out, preferred_element_type=jnp.float32
    ).reshape(person_rows, frame_rows, width)
    return (stream + branch).astype(jnp.bfloat16)


def solution(mesh):
    placed = (
        P(("groups", "person"), "frame", None),
        P(),
        P(),
        P(),
        P(),
        P(),
        P(),
        P("frame", None),
        P(),
        P(),
        P("frame", None),
        P("groups"),
        P("groups"),
    )
    return jax.shard_map(
        on_device,
        mesh=mesh,
        in_specs=placed,
        out_specs=P(("groups", "person"), "frame", None),
        check_vma=False,
    )
```

profile of v0, /device:TPU:0, one launch (start us, length us, event | category | flops | bytes accessed | tf_op | source)
XLA Modules:
  0.0 269.7 jit_solution(962375426312718564)
XLA Ops:
  10.8 6.3 %all-to-all-start.1 = ((s32[4,1,1024]{2,1,0:T(1,128)}), s32[4,1,1024]{2,1,0:T(1,128)S(1)}, u32[]{:S(2)}, u32[]{:S(2)}) async-start(s32[4,1,1024]{2,1,0:T(1,128)} %reshape.196), calls=%async_computation.1 | async-start | bytes 32768 | tf_op jit(solution)/shard_map/all_to_all | solution.py:78
  17.1 8.9 %copy.114 = bf16[1024,3072]{0,1:T(8,128)(2,1)} copy(bf16[1024,3072]{1,0:T(8,128)(2,1)} %param.17) | data formatting | bytes 12582912 | tf_op args[2]
  26.2 6.3 %fusion.41 = f32[4,64,3,16,64]{1,4,3,2,0:T(8,128)S(1)} fusion(bf16[3,16,64,1024,1]{3,2,1,0,4:T(8,128)(2,1)} %bitcast.204, bf16[4,64,1024]{2,1,0:T(8,128)(2,1)S(1)} %copy-done.5, f32[1024]{0:T(1024)S(1)} %copy-done.11, f32[4,64]{1,0:T(4,128)S(1)} %add_rsqrt_fusion.5), kind=kOutput, calls=%fused_computation.60 | convolution fusion | flops 1611661312 | bytes 9966592 | tf_op jit(solution)/shard_map/dot_general | solution.py:19
  33.4 2.2 multiply_convert_fusion.2
  35.7 1.6 reshape.198
  37.2 5.1 %all-to-all-start.2 = ((bf16[4,2,32768]{2,1,0:T(2,128)(2,1)}), bf16[4,2,32768]{2,1,0:T(2,128)(2,1)}, u32[]{:S(2)}, u32[]{:S(2)}) async-start(bf16[4,2,32768]{2,1,0:T(2,128)(2,1)} %reshape.198), calls=%async_computation.2 | async-start | bytes 1048576 | tf_op jit(solution)/shard_map/all_to_all | solution.py:75
  42.3 1.3 copy.157
  43.6 1.6 reshape.200
  45.2 26.6 %all-to-all-done.2 = bf16[4,2,32768]{2,1,0:T(2,128)(2,1)} async-done(((bf16[4,2,32768]{2,1,0:T(2,128)(2,1)}), bf16[4,2,32768]{2,1,0:T(2,128)(2,1)}, u32[]{:S(2)}, u32[]{:S(2)}) %all-to-all-start.2) | async-done | bytes 524320 | tf_op jit(solution)/shard_map/all_to_all | solution.py:75
  71.8 4.1 %all-to-all-start.3 = ((bf16[4,2,32768]{2,1,0:T(2,128)(2,1)}), bf16[4,2,32768]{2,1,0:T(2,128)(2,1)}, u32[]{:S(2)}, u32[]{:S(2)}) async-start(bf16[4,2,32768]{2,1,0:T(2,128)(2,1)} %reshape.200), calls=%async_computation.3 | async-start | bytes 1048576 | tf_op jit(solution)/shard_map/all_to_all | solution.py:76
  75.9 1.8 copy_bitcast_fusion.7
  77.7 1.6 reshape.194
  79.3 22.0 %all-to-all-done.3 = bf16[4,2,32768]{2,1,0:T(2,128)(2,1)} async-done(((bf16[4,2,32768]{2,1,0:T(2,128)(2,1)}), bf16[4,2,32768]{2,1,0:T(2,128)(2,1)}, u32[]{:S(2)}, u32[]{:S(2)}) %all-to-all-start.3) | async-done | bytes 524320 | tf_op jit(solution)/shard_map/all_to_all | solution.py:76
  101.3 6.8 %all-to-all-start = ((bf16[4,2,32768]{2,1,0:T(2,128)(2,1)}), bf16[4,2,32768]{2,1,0:T(2,128)(2,1)}, u32[]{:S(2)}, u32[]{:S(2)}) async-start(bf16[4,2,32768]{2,1,0:T(2,128)(2,1)} %reshape.194), calls=%async_computation | async-start | bytes 1048576 | tf_op jit(solution)/shard_map/all_to_all | solution.py:77
  109.0 1.7 reshape.199
  110.8 1.9 copy.120
  112.6 2.7 %all_to_all.137 = bf16[4,256,4,64]{1,3,2,0:T(8,128)(2,1)} reshape(bf16[4,4,64,4,64]{2,1,4,3,0:T(4,128)(2,1)} %copy.120) | data formatting | bytes 1048576 | tf_op jit(solution)/shard_map/all_to_all | solution.py:75
  115.4 1.7 reshape.201
  117.1 1.9 copy.122
  119.0 2.8 %all_to_all.141 = bf16[4,256,4,64]{1,3,2,0:T(8,128)(2,1)} reshape(bf16[4,4,64,4,64]{2,1,4,3,0:T(4,128)(2,1)} %copy.122) | data formatting | bytes 1048576 | tf_op jit(solution)/shard_map/all_to_all | solution.py:76
  121.7 12.9 %all-to-all-done = bf16[4,2,32768]{2,1,0:T(2,128)(2,1)} async-done(((bf16[4,2,32768]{2,1,0:T(2,128)(2,1)}), bf16[4,2,32768]{2,1,0:T(2,128)(2,1)}, u32[]{:S(2)}, u32[]{:S(2)}) %all-to-all-start) | async-done | bytes 524320 | tf_op jit(solution)/shard_map/all_to_all | solution.py:77
  134.6 1.7 reshape.195
  136.4 1.9 copy.116
  138.2 2.1 all_to_all.129
  140.3 9.1 %while.10 = (s32[]{:T(128)}, bf16[4,256,4,64]{1,3,2,0:T(8,128)(2,1)}, bf16[4,256,4,64]{1,3,2,0:T(8,128)(2,1)S(1)}, s32[4,256,4,1]{1,3,2,0:T(1,128)S(1)}, bf16[4,...) while((s32[]{:T(128)}, bf16[4,256,4,64]{1,3,2,0:T(8,128)(2,1)}, ...), condition=%wide.region_5.6_spmd, body=%wide.region_3.5_spmd.sunk | while | flops 68287744 | bytes 1592913 | solution.py:72
  140.4 1.4 convert_reduce_fusion.3
  141.7 0.9 fusion.66
  142.6 1.4 convert_reduce_fusion.3
  144.0 0.9 fusion.66
  144.9 1.4 convert_reduce_fusion.3
  146.3 0.9 fusion.66
  147.2 1.4 convert_reduce_fusion.3
  148.5 0.9 fusion.66
  149.4 1.8 copy.124
  151.2 1.6 reshape.202
  152.8 7.1 %all-to-all-start.4 = ((bf16[4,2,32768]{2,1,0:T(2,128)(2,1)}), bf16[4,2,32768]{2,1,0:T(2,128)(2,1)S(1)}, u32[]{:S(2)}, u32[]{:S(2)}) async-start(bf16[4,2,32768]{2,1,0:T(2,128)(2,1)} %reshape.202), calls=%async_computation.4 | async-start | bytes 1048576 | tf_op jit(solution)/shard_map/all_to_all | solution.py:81
  162.1 9.3 %all-to-all-done.4 = bf16[4,2,32768]{2,1,0:T(2,128)(2,1)S(1)} async-done(((bf16[4,2,32768]{2,1,0:T(2,128)(2,1)}), bf16[4,2,32768]{2,1,0:T(2,128)(2,1)S(1)}, u32[]{:S(2)}, u32[]{:S(2)}) %all-to-all-start.4) | async-done | bytes 524320 | tf_op jit(solution)/shard_map/all_to_all | solution.py:81
  172.1 3.5 %all-to-all-start.6 = ((s32[4,1,1024]{2,1,0:T(1,128)}), s32[4,1,1024]{2,1,0:T(1,128)S(1)}, u32[]{:S(2)}, u32[]{:S(2)}) async-start(s32[4,1,1024]{2,1,0:T(1,128)} %reshape.208), calls=%async_computation.6 | async-start | bytes 32768 | tf_op jit(solution)/shard_map/all_to_all | solution.py:97
  175.6 1.7 reshape.203
  177.4 1.4 copy.154
  178.7 2.4 dot_general.39
  181.1 1.8 fusion.23
  183.1 8.6 %copy.126 = bf16[3072,1024]{1,0:T(8,128)(2,1)} copy(bf16[3072,1024]{0,1:T(8,128)(2,1)} %bitcast.203) | data formatting | bytes 12582912 | tf_op jit(solution)/shard_map/dot_general | solution.py:19
  191.8 6.3 %fusion.38 = f32[4,64,3,16,64]{1,4,3,2,0:T(8,128)S(1)} fusion(bf16[3,16,64,1024,1]{3,2,1,0,4:T(8,128)(2,1)} %bitcast.205, bf16[4,64,1024]{2,1,0:T(8,128)(2,1)S(1)} %fusion.23, f32[1024]{0:T(1024)S(1)} %copy-done.12, f32[4,64]{1,0:T(4,128)S(1)} %add_rsqrt_fusion.4), kind=kOutput, calls=%fused_computation.58 | convolution fusion | flops 1611661312 | bytes 9966592 | tf_op jit(solution)/shard_map/dot_general | solution.py:19
  200.8 1.5 reshape.204
  202.3 3.5 %all-to-all-start.7 = ((bf16[4,2,32768]{2,1,0:T(2,128)(2,1)}), bf16[4,2,32768]{2,1,0:T(2,128)(2,1)S(1)}, u32[]{:S(2)}, u32[]{:S(2)}) async-start(bf16[4,2,32768]{2,1,0:T(2,128)(2,1)} %reshape.204), calls=%async_computation.7 | async-start | bytes 1048576 | tf_op jit(solution)/shard_map/all_to_all | solution.py:94
  206.7 1.5 reshape.206
  208.2 6.3 %all-to-all-done.7 = bf16[4,2,32768]{2,1,0:T(2,128)(2,1)S(1)} async-done(((bf16[4,2,32768]{2,1,0:T(2,128)(2,1)}), bf16[4,2,32768]{2,1,0:T(2,128)(2,1)S(1)}, u32[]{:S(2)}, u32[]{:S(2)}) %all-to-all-start.7) | async-done | bytes 524320 | tf_op jit(solution)/shard_map/all_to_all | solution.py:94
  214.6 3.5 %all-to-all-start.8 = ((bf16[4,2,32768]{2,1,0:T(2,128)(2,1)}), bf16[4,2,32768]{2,1,0:T(2,128)(2,1)S(1)}, u32[]{:S(2)}, u32[]{:S(2)}) async-start(bf16[4,2,32768]{2,1,0:T(2,128)(2,1)} %reshape.206), calls=%async_computation.8 | async-start | bytes 1048576 | tf_op jit(solution)/shard_map/all_to_all | solution.py:95
  218.2 1.8 copy_bitcast_fusion.4
  220.0 1.5 reshape.210
  222.2 1.6 copy.133
  223.9 3.0 %all-to-all-done.8 = bf16[4,2,32768]{2,1,0:T(2,128)(2,1)S(1)} async-done(((bf16[4,2,32768]{2,1,0:T(2,128)(2,1)}), bf16[4,2,32768]{2,1,0:T(2,128)(2,1)S(1)}, u32[]{:S(2)}, u32[]{:S(2)}) %all-to-all-start.8) | async-done | bytes 524320 | tf_op jit(solution)/shard_map/all_to_all | solution.py:95
  226.9 4.4 %all-to-all-start.5 = ((bf16[4,2,32768]{2,1,0:T(2,128)(2,1)}), bf16[4,2,32768]{2,1,0:T(2,128)(2,1)}, u32[]{:S(2)}, u32[]{:S(2)}) async-start(bf16[4,2,32768]{2,1,0:T(2,128)(2,1)} %reshape.210), calls=%async_computation.5 | async-start | bytes 1048576 | tf_op jit(solution)/shard_map/all_to_all | solution.py:96
  232.0 2.4 copy.135
  234.4 1.9 fusion.49
  236.3 1.3 copy.136
  237.8 1.7 copy.137
  239.9 1.7 reshape.211
  241.7 1.6 copy.128
  243.3 0.9 fusion.16
  245.6 11.4 %all_to_all.175 = bf16[4,2,32768]{2,1,0:T(2,128)(2,1)S(1)} all-to-all(bf16[4,2,32768]{2,1,0:T(2,128)(2,1)S(1)} %reshape.212), channel_id=1, replica_groups=mesh['groups'=2,'person'=4,'frame'=4] {'person'}, dimensions={0} | all-to-all | bytes 1048576 | tf_op jit(solution)/shard_map/all_to_all | solution.py:107
  258.0 1.5 dot_general.46
  259.6 3.3 %fusion.26 = bf16[4,64,1024]{2,1,0:T(8,128)(2,1)} fusion(bf16[4,64,1024]{2,1,0:T(8,128)(2,1)} %dot_general.46, bf16[1024,1024]{1,0:T(8,128)(2,1)} %all-gather.5.cloned.1.call-done, bf16[4,64,1024]{2,1,0:T(8,128)(2,1)} %copy-done.6), kind=kOutput, calls=%fused_computation.46 | convolution fusion | flops 537657344 | bytes 3670016 | tf_op jit(solution)/shard_map/dot_general | solution.py:108
  (88 shorter events, 17.5 us)
Async XLA Ops:
  6.5 174.6 %copy-start = (bf16[1024,1024]{1,0:T(8,128)(2,1)S(1)}, bf16[1024,1024]{1,0:T(8,128)(2,1)}, u32[]{:S(2)}) copy-start(bf16[1024,1024]{1,0:T(8,128)(2,1)} %param.20) | copy-start | bytes 6291460
  6.5 176.6 %all-gather.3.cloned.1.call-start = ((), (), s32[]{:S(2)}) async-start(), calls=%async_computation.10 | async-start | bytes 7864320 | tf_op jit(solution)/shard_map/all_gather | solution.py:47
  10.8 26.4 %all-to-all-start.1 = ((s32[4,1,1024]{2,1,0:T(1,128)}), s32[4,1,1024]{2,1,0:T(1,128)S(1)}, u32[]{:S(2)}, u32[]{:S(2)}) async-start(s32[4,1,1024]{2,1,0:T(1,128)} %reshape.196), calls=%async_computation.1 | async-start | bytes 32768 | tf_op jit(solution)/shard_map/all_to_all | solution.py:78
  17.1 8.9 %copy-start.5 = (bf16[4,64,1024]{2,1,0:T(8,128)(2,1)S(1)}, bf16[4,64,1024]{2,1,0:T(8,128)(2,1)}, u32[]{:S(2)}) copy-start(bf16[4,64,1024]{2,1,0:T(8,128)(2,1)} %param.15) | copy-start | bytes 1572868
  17.1 9.1 %copy-start.11 = (f32[1024]{0:T(1024)S(1)}, f32[1024]{0:T(1024)}, u32[]{:S(2)}) copy-start(f32[1024]{0:T(1024)} %param.16) | copy-start | bytes 12292
  32.5 3.1 %copy-start.3 = (f32[4,64,3,16,64]{1,4,3,2,0:T(8,128)}, f32[4,64,3,16,64]{1,4,3,2,0:T(8,128)S(1)}, u32[]{:S(2)}) copy-start(f32[4,64,3,16,64]{1,4,3,2,0:T(8,128)S(1)} %fusion.41) | copy-start | bytes 9437188
  32.6 0.8 copy-start.7
  32.6 0.8 copy-start.8
  37.2 34.5 %all-to-all-start.2 = ((bf16[4,2,32768]{2,1,0:T(2,128)(2,1)}), bf16[4,2,32768]{2,1,0:T(2,128)(2,1)}, u32[]{:S(2)}, u32[]{:S(2)}) async-start(bf16[4,2,32768]{2,1,0:T(2,128)(2,1)} %reshape.198), calls=%async_computation.2 | async-start | bytes 1048576 | tf_op jit(solution)/shard_map/all_to_all | solution.py:75
  71.8 29.5 %all-to-all-start.3 = ((bf16[4,2,32768]{2,1,0:T(2,128)(2,1)}), bf16[4,2,32768]{2,1,0:T(2,128)(2,1)}, u32[]{:S(2)}, u32[]{:S(2)}) async-start(bf16[4,2,32768]{2,1,0:T(2,128)(2,1)} %reshape.200), calls=%async_computation.3 | async-start | bytes 1048576 | tf_op jit(solution)/shard_map/all_to_all | solution.py:76
  101.3 33.3 %all-to-all-start = ((bf16[4,2,32768]{2,1,0:T(2,128)(2,1)}), bf16[4,2,32768]{2,1,0:T(2,128)(2,1)}, u32[]{:S(2)}, u32[]{:S(2)}) async-start(bf16[4,2,32768]{2,1,0:T(2,128)(2,1)} %reshape.194), calls=%async_computation | async-start | bytes 1048576 | tf_op jit(solution)/shard_map/all_to_all | solution.py:77
  152.8 18.6 %all-to-all-start.4 = ((bf16[4,2,32768]{2,1,0:T(2,128)(2,1)}), bf16[4,2,32768]{2,1,0:T(2,128)(2,1)S(1)}, u32[]{:S(2)}, u32[]{:S(2)}) async-start(bf16[4,2,32768]{2,1,0:T(2,128)(2,1)} %reshape.202), calls=%async_computation.4 | async-start | bytes 1048576 | tf_op jit(solution)/shard_map/all_to_all | solution.py:81
  159.9 99.7 %all-gather.5.cloned.1.call-start = ((), (), s32[]{:S(2)}) async-start(), calls=%async_computation.11 | async-start | bytes 2621440 | tf_op jit(solution)/shard_map/all_gather | solution.py:48
  171.4 0.8 copy-start.4
  172.1 30.1 %all-to-all-start.6 = ((s32[4,1,1024]{2,1,0:T(1,128)}), s32[4,1,1024]{2,1,0:T(1,128)S(1)}, u32[]{:S(2)}, u32[]{:S(2)}) async-start(s32[4,1,1024]{2,1,0:T(1,128)} %reshape.208), calls=%async_computation.6 | async-start | bytes 32768 | tf_op jit(solution)/shard_map/all_to_all | solution.py:97
  182.9 8.9 %copy-start.6 = (bf16[4,64,1024]{2,1,0:T(8,128)(2,1)}, bf16[4,64,1024]{2,1,0:T(8,128)(2,1)S(1)}, u32[]{:S(2)}) copy-start(bf16[4,64,1024]{2,1,0:T(8,128)(2,1)S(1)} %fusion.23) | copy-start | bytes 1572868
  183.1 8.7 %copy-start.12 = (f32[1024]{0:T(1024)S(1)}, f32[1024]{0:T(1024)}, u32[]{:S(2)}) copy-start(f32[1024]{0:T(1024)} %param.21) | copy-start | bytes 12292
  198.1 2.7 copy-start.2
  198.1 0.9 copy-start.9
  198.1 0.9 copy-start.10
  202.3 12.3 %all-to-all-start.7 = ((bf16[4,2,32768]{2,1,0:T(2,128)(2,1)}), bf16[4,2,32768]{2,1,0:T(2,128)(2,1)S(1)}, u32[]{:S(2)}, u32[]{:S(2)}) async-start(bf16[4,2,32768]{2,1,0:T(2,128)(2,1)} %reshape.204), calls=%async_computation.7 | async-start | bytes 1048576 | tf_op jit(solution)/shard_map/all_to_all | solution.py:94
  214.6 12.3 %all-to-all-start.8 = ((bf16[4,2,32768]{2,1,0:T(2,128)(2,1)}), bf16[4,2,32768]{2,1,0:T(2,128)(2,1)S(1)}, u32[]{:S(2)}, u32[]{:S(2)}) async-start(bf16[4,2,32768]{2,1,0:T(2,128)(2,1)} %reshape.206), calls=%async_computation.8 | async-start | bytes 1048576 | tf_op jit(solution)/shard_map/all_to_all | solution.py:95
  226.9 13.1 %all-to-all-start.5 = ((bf16[4,2,32768]{2,1,0:T(2,128)(2,1)}), bf16[4,2,32768]{2,1,0:T(2,128)(2,1)}, u32[]{:S(2)}, u32[]{:S(2)}) async-start(bf16[4,2,32768]{2,1,0:T(2,128)(2,1)} %reshape.210), calls=%async_computation.5 | async-start | bytes 1048576 | tf_op jit(solution)/shard_map/all_to_all | solution.py:96
  258.0 4.9 %copy-start.1 = (bf16[1024,1024]{1,0:T(8,128)(2,1)S(1)}, bf16[1024,1024]{1,0:T(8,128)(2,1)}, u32[]{:S(2)}) copy-start(bf16[1024,1024]{1,0:T(8,128)(2,1)} %param.20) | copy-start | bytes 6291460
Sparse Core Ops, SparseCore 0:
  8.9 153.4 all-gather.2
  164.0 45.8 all-gather.4
where the time goes:
time: 271 us; the launch traced here: 270 us
  waiting for transfers between devices  81.7 us (30%)
  local copies, waits for them, and re-layouts  80 us (30%)
  starting transfers between devices  44.3 us (16%)
  matrix products  29.4 us (11%)
  between operations  14 us (5%)
  blocking collectives  11.4 us (4%)
  other arithmetic  8.98 us (3%)
    unnamed x52, local copies, waits for them, and re-layouts  38.9 us
    all_to_all x1, waiting for transfers between devices, on_device(): lax.all_to_all(queries, 'frame', split_axis=2, concat_axis=1, tiled=True)  26.6 us
    all_to_all x1, waiting for transfers between devices, on_device(): lax.all_to_all(key_rows, 'frame', split_axis=2, concat_axis=1, tiled=True)  22 us
    all_to_all x1, waiting for transfers between devices, on_device(): lax.all_to_all(value_rows, 'frame', split_axis=2, concat_axis=1, tiled=True)  12.9 us
    dot_general x2, matrix products, project(): jnp.dot(flat_rows, weight, preferred_element_type=jnp.float32)  12.6 us
    all_to_all x1, blocking collectives, on_device(): lax.all_to_all(results, 'person', split_axis=0, concat_axis=2, tiled=True)  11.4 us
    all_to_all x1, waiting for transfers between devices, on_device(): lax.all_to_all(results, 'frame', split_axis=1, concat_axis=2, tiled=True)  9.29 us
    dot_general x1, local copies, waits for them, and re-layouts, project(): jnp.dot(flat_rows, weight, preferred_element_type=jnp.float32)  8.65 us
  transfers between devices with their start and end apart: 11, of which 7 were waited for; matrix products, arithmetic and copies ran while one was open for 39% of the time, Pallas kernels for 0%

commit v1 on v0

--- a/solution.py
+++ b/solution.py
@@ -1,12 +1,414 @@
+import functools
 import math
 
 import jax
 import jax.numpy as jnp
 from jax import lax
+from jax.experimental import pallas as pl
+from jax.experimental.pallas import tpu as pltpu
 from jax.sharding import PartitionSpec as P
 
 H = 16
 HD = 64
+MESH = pl.DeviceIdType.MESH
+F32 = jnp.float32
+BF16 = jnp.bfloat16
+
+
+def block_kernel(
+    counts,
+    present,
+    tokens,
+    norm_time,
+    qkv_time,
+    gain_time,
+    out_time,
+    norm_cross,
+    qkv_cross,
+    gain_cross,
+    out_cross,
+    out,
+    tok,
+    w_time,
+    wo_time,
+    w_cross,
+    hid,
+    att,
+    bias,
+    mid,
+    mid_in,
+    res,
+    local_sem,
+    tok_send,
+    tok_recv,
+    z_send,
+    z_recv,
+    hop_send,
+    hop_recv,
+    mid_send,
+    mid_recv,
+    out_send,
+    out_recv,
+):
+    nz, nx = 4, 4
+    group = lax.axis_index("groups")
+    xc = lax.axis_index("person")
+    z = lax.axis_index("frame")
+    x, core = xc // 2, xc % 2
+    rows, width = hid.shape
+    frames = tok.shape[1]
+    depth = qkv_cross.shape[0]
+    piece = depth // 16
+    part = frames // nx
+
+    def zs(d):
+        return (z - d + nz) % nz
+
+    def zt(d):
+        return (z + d) % nz
+
+    def xs(i):
+        return (xc - i + nx) % nx
+
+    def xt(i):
+        return (xc + i) % nx
+
+    barrier = pltpu.get_barrier_semaphore()
+    for i in range(nx):
+        for d in range(nz):
+            if i or d:
+                pl.semaphore_signal(
+                    barrier, inc=1, device_id={"person": xt(i), "frame": zt(d)}, device_id_type=MESH
+                )
+    pl.semaphore_signal(barrier, inc=1, device_id={"groups": 1 - group}, device_id_type=MESH)
+    own = pl.multiple_of(z * depth, depth)
+    local = [
+        pltpu.make_async_copy(tokens.at[z], tok.at[z], local_sem.at[0]),
+        pltpu.make_async_copy(qkv_time, w_time, local_sem.at[1]),
+        pltpu.make_async_copy(out_time, wo_time, local_sem.at[2]),
+        pltpu.make_async_copy(
+            qkv_cross, w_cross.at[pl.ds(own, depth), pl.ds(0, 3 * width)], local_sem.at[3]
+        ),
+        pltpu.make_async_copy(
+            out_cross, w_cross.at[pl.ds(own, depth), pl.ds(3 * width, width)], local_sem.at[4]
+        ),
+    ]
+    for copy in local:
+        copy.start()
+    pl.semaphore_wait(barrier, nx * nz)
+
+    def tok_copy(block, slot, d, peer):
+        return pltpu.make_async_remote_copy(
+            src_ref=tokens.at[block],
+            dst_ref=tok.at[slot],
+            send_sem=tok_send.at[d - 1],
+            recv_sem=tok_recv.at[d - 1],
+            device_id={"frame": peer},
+            device_id_type=MESH,
+        )
+
+    for d in (2, 1, 3):
+        tok_copy(zt(d), z, d, zt(d)).start()
+
+    def at_piece(half):
+        slot = core * 4 + (group * 2 + x if half == 0 else x * 2 + group)
+        return half * (depth // 2) + slot * piece
+
+    def z_copy(half, d, array, source, peer):
+        start = pl.multiple_of(at_piece(half), piece)
+        into = pl.multiple_of(source * depth + at_piece(half), piece)
+        ref = (qkv_cross, out_cross)[array]
+        columns = (pl.ds(0, 3 * width), pl.ds(3 * width, width))[array]
+        return pltpu.make_async_remote_copy(
+            src_ref=ref.at[pl.ds(start, piece), :],
+            dst_ref=w_cross.at[pl.ds(into, piece), columns],
+            send_sem=z_send.at[half, d - 1, array],
+            recv_sem=z_recv.at[half, d - 1, array],
+            device_id={"frame": peer},
+            device_id_type=MESH,
+        )
+
+    for d in (1, 3, 2):
+        for half in range(2):
+            for array in range(2):
+                z_copy(half, d, array, z, zt(d)).start()
+
+    def hop_copy(hop, half, d, incoming):
+        along_x = (half == 0) == (hop == 0)
+        if hop == 2:
+            side = 1 - core if incoming else core
+            offset, length = side * 4, 4
+            device = {"person": x * 2 + 1 - core}
+        else:
+            gx = (1 - x if incoming and along_x else x)
+            gy = (1 - group if incoming and not along_x else group)
+            if hop == 0:
+                offset, length = core * 4 + (gy * 2 + gx if half == 0 else gx * 2 + gy), 1
+            else:
+                offset, length = core * 4 + (gy if half == 0 else gx) * 2, 2
+            device = {"person": (1 - x) * 2 + core} if along_x else {"groups": 1 - group}
+        start = pl.multiple_of(
+            zs(d) * depth + half * (depth // 2) + offset * piece, length * piece
+        )
+        block = w_cross.at[pl.ds(start, length * piece), :]
+        return pltpu.make_async_remote_copy(
+            src_ref=block,
+            dst_ref=block,
+            send_sem=hop_send.at[hop, half, d - 1],
+            recv_sem=hop_recv.at[hop, half, d - 1],
+            device_id=device,
+            device_id_type=MESH,
+        )
+
+    def forward(hop, d):
+        for half in range(2):
+            if hop == 0:
+                for array in range(2):
+                    z_copy(half, d, array, zs(d), zs(d)).wait_recv()
+            else:
+                hop_copy(hop - 1, half, d, True).wait_recv()
+        for half in range(2):
+            hop_copy(hop, half, d, False).start()
+
+    lane = lax.broadcasted_iota(jnp.int32, (rows, 128), 1)
+    low = lane < HD
+    same_head = (
+        lax.broadcasted_iota(jnp.int32, (256, 256), 0) // HD
+        == lax.broadcasted_iota(jnp.int32, (256, 256), 1) // HD
+    )
+    blocks = jnp.where(same_head, 1.0, 0.0).astype(BF16)
+    ones = jnp.ones((rows, 128), BF16)
+    key_index = lax.broadcasted_iota(jnp.int32, (rows, rows), 1)
+    query_index = lax.broadcasted_iota(jnp.int32, (rows, rows), 0)
+
+    def normed(stream, gains):
+        scale = lax.rsqrt(jnp.mean(stream * stream, axis=-1, keepdims=True) + 1e-06)
+        return (stream * scale * gains).astype(BF16)
+
+    def attend(weight, gain):
+        hidden = hid[...]
+
+        def project(column):
+            return jnp.dot(hidden, weight[:, pl.ds(column, 256)], preferred_element_type=F32)
+
+        def unit(entries):
+            squares = jnp.dot((entries * entries).astype(BF16), blocks, preferred_element_type=F32)
+            return entries * lax.rsqrt(squares * (1.0 / HD) + 1e-06)
+
+        def step(t, carry):
+            column = pl.multiple_of(t * 256, 256)
+            queries = unit(project(column)) * gain[...]
+            keys = unit(project(width + column)).astype(BF16)
+            values = project(2 * width + column).astype(BF16)
+            for pair in range(2):
+                lanes = slice(pair * 128, (pair + 1) * 128)
+                two = queries[:, lanes]
+                extended = jnp.concatenate([values[:, lanes], ones], axis=1)
+                sums = []
+                for member in range(2):
+                    one = jnp.where(low if member == 0 else ~low, two, 0.0).astype(BF16)
+                    scores = lax.dot_general(
+                        one, keys[:, lanes], (((1,), (1,)), ((), ())), preferred_element_type=F32
+                    )
+                    weights = jnp.exp(scores + bias[...]).astype(BF16)
+                    sums.append(jnp.dot(weights, extended, preferred_element_type=F32))
+                summed = jnp.where(low, sums[0][:, :128], sums[1][:, :128])
+                total = jnp.where(low, sums[0][:, 128:], sums[1][:, 128:])
+                att[:, pl.ds(column + pair * 128, 128)] = (summed / total).astype(BF16)
+            return carry
+
+        lax.fori_loop(0, width // 256, step, 0)
+
+    person = xc * nz + z
+    bias[...] = jnp.where(key_index < counts[person], 0.0, -1e30)
+    local[0].wait()
+    for d in (1, 3, 2):
+        tok_copy(zs(d), zs(d), d, zs(d)).wait_recv()
+    hid[...] = normed(tok[...].reshape(rows, width).astype(F32), norm_time[...])
+    local[1].wait()
+    attend(w_time, gain_time)
+    local[2].wait()
+
+    def temporal_out(t, carry):
+        column = pl.multiple_of(t * 256, 256)
+        branch = jnp.dot(att[...], wo_time[:, pl.ds(column, 256)], preferred_element_type=F32)
+        stream = tok[:, :, pl.ds(column, 256)].reshape(rows, 256).astype(F32)
+        mid[:, pl.ds(column, 256)] = (stream + branch).astype(BF16)
+        return carry
+
+    lax.fori_loop(0, width // 256, temporal_out, 0)
+
+    def mid_copy(i, d, take_x, take_z, owner, peer):
+        start = pl.multiple_of(take_z * frames + take_x * part, part)
+        into = pl.multiple_of(owner * part, part)
+        return pltpu.make_async_remote_copy(
+            src_ref=mid.at[pl.ds(start, part), :],
+            dst_ref=mid_in.at[pl.ds(into, part), :],
+            send_sem=mid_send.at[i, d],
+            recv_sem=mid_recv.at[i, d],
+            device_id=peer,
+            device_id_type=MESH,
+        )
+
+    offsets = [(i, d) for d in (2, 1, 3, 0) for i in range(nx) if i or d]
+    for i, d in offsets:
+        mid_copy(i, d, xt(i), zt(d), person, {"person": xt(i), "frame": zt(d)}).start()
+    into = pl.multiple_of(person * part, part)
+    start = pl.multiple_of(z * frames + xc * part, part)
+    mid_in[pl.ds(into, part), :] = mid[pl.ds(start, part), :]
+
+    for d in (1, 3, 2):
+        forward(0, d)
+
+    key_row = lax.broadcasted_iota(jnp.int32, (8, rows), 1)
+    limit = jnp.zeros((8, rows), jnp.int32)
+    for member in range(nx * nz):
+        valid = jnp.where(present[member] == 1, counts[member], 0)
+        limit = jnp.where(key_row // part == member, valid, limit)
+    frame = z * frames + xc * part + key_row % part
+    usable = jnp.broadcast_to(jnp.where(frame < limit, 1, 0)[:1, :], (rows, rows))
+    allowed = ((key_index % part == query_index % part) & (usable > 0)) | (key_index == query_index)
+    bias[...] = jnp.where(allowed, 0.0, -1e30)
+
+    for d in (1, 3, 2):
+        forward(1, d)
+    for i, d in offsets:
+        source = xs(i) * nz + zs(d)
+        mid_copy(i, d, xc, z, source, {"person": xs(i), "frame": zs(d)}).wait_recv()
+    hid[...] = normed(mid_in[...].astype(F32), norm_cross[...])
+    for d in (1, 3, 2):
+        forward(2, d)
+    local[3].wait()
+    local[4].wait()
+    for d in (1, 3, 2):
+        for half in range(2):
+            hop_copy(2, half, d, True).wait_recv()
+    attend(w_cross, gain_cross)
+
+    def cross_out(t, carry):
+        column = pl.multiple_of(t * 256, 256)
+        branch = jnp.dot(
+            att[...], w_cross[:, pl.ds(3 * width + column, 256)], preferred_element_type=F32
+        )
+        total = mid_in[:, pl.ds(column, 256)].astype(F32) + branch
+        res[:, :, pl.ds(column, 256)] = total.astype(BF16).reshape(nx * nz, part, 256)
+        return carry
+
+    lax.fori_loop(0, width // 256, cross_out, 0)
+
+    def out_copy(i, block, slot, peer):
+        return pltpu.make_async_remote_copy(
+            src_ref=res.at[pl.ds(block * nz, nz)],
+            dst_ref=out.at[:, pl.ds(pl.multiple_of(slot * part, part), part), :],
+            send_sem=out_send.at[i - 1],
+            recv_sem=out_recv.at[i - 1],
+            device_id={"person": peer},
+            device_id_type=MESH,
+        )
+
+    for i in (2, 3, 1):
+        out_copy(i, xt(i), xc, xt(i)).start()
+    kept = pltpu.make_async_copy(
+        res.at[pl.ds(xc * nz, nz)],
+        out.at[:, pl.ds(pl.multiple_of(xc * part, part), part), :],
+        local_sem.at[5],
+    )
+    kept.start()
+    for d in (1, 2, 3):
+        tok_copy(zt(d), z, d, zt(d)).wait_send()
+        for half in range(2):
+            for array in range(2):
+                z_copy(half, d, array, z, zt(d)).wait_send()
+            for hop in range(3):
+                hop_copy(hop, half, d, False).wait_send()
+    for i, d in offsets:
+        mid_copy(i, d, xt(i), zt(d), person, {"person": xt(i), "frame": zt(d)}).wait_send()
+    kept.wait()
+    for i in (1, 2, 3):
+        out_copy(i, xt(i), xc, xt(i)).wait_send()
+        out_copy(i, xs(i), xs(i), xs(i)).wait_recv()
+
+
+def whole_block(
+    tokens,
+    norm_time,
+    qkv_time,
+    qgain_time,
+    kgain_time,
+    out_time,
+    norm_cross,
+    qkv_cross,
+    qgain_cross,
+    kgain_cross,
+    out_cross,
+    frame_counts,
+    presence,
+):
+    persons, frames, width = tokens.shape
+    rows = persons * frames
+    scale = 3.0 / math.sqrt(HD)
+    gain_time = jnp.tile(qgain_time * kgain_time * scale, 4)[None, :]
+    gain_cross = jnp.tile(qgain_cross * kgain_cross * scale, 4)[None, :]
+    smem = pl.BlockSpec(memory_space=pltpu.SMEM)
+    vmem = pl.BlockSpec(memory_space=pltpu.VMEM)
+    anywhere = pl.BlockSpec(memory_space=pl.ANY)
+    dma = pltpu.SemaphoreType.DMA
+    return pl.pallas_call(
+        block_kernel,
+        out_shape=jax.ShapeDtypeStruct(tokens.shape, BF16),
+        in_specs=[
+            smem,
+            smem,
+            anywhere,
+            vmem,
+            anywhere,
+            vmem,
+            anywhere,
+            vmem,
+            anywhere,
+            vmem,
+            anywhere,
+        ],
+        out_specs=anywhere,
+        scratch_shapes=[
+            pltpu.VMEM(tokens.shape, BF16),
+            pltpu.VMEM((width, 3 * width), BF16),
+            pltpu.VMEM((width, width), BF16),
+            pltpu.VMEM((width, 4 * width), BF16),
+            pltpu.VMEM((rows, width), BF16),
+            pltpu.VMEM((rows, width), BF16),
+            pltpu.VMEM((rows, rows), F32),
+            pltpu.VMEM((rows, width), BF16),
+            pltpu.VMEM((rows, width), BF16),
+            pltpu.VMEM((16, rows // 16, width), BF16),
+            dma((6,)),
+            dma((3,)),
+            dma((3,)),
+            dma((2, 3, 2)),
+            dma((2, 3, 2)),
+            dma((3, 2, 3)),
+            dma((3, 2, 3)),
+            dma((4, 4)),
+            dma((4, 4)),
+            dma((3,)),
+            dma((3,)),
+        ],
+        compiler_params=pltpu.CompilerParams(
+            collective_id=0, has_side_effects=True, vmem_limit_bytes=48 * 1024 * 1024
+        ),
+    )(
+        frame_counts,
+        presence,
+        tokens,
+        norm_time[None, :],
+        qkv_time,
+        gain_time,
+        out_time,
+        norm_cross[None, :],
+        qkv_cross,
+        gain_cross,
+        out_cross,
+    )
 
 
 def norm_rows(entries, gains):
@@ -127,8 +529,10 @@
         P("groups"),
         P("groups"),
     )
+    sizes = dict(mesh.shape)
+    fits = sizes == {"groups": 2, "person": 4, "frame": 4}
     return jax.shard_map(
-        on_device,
+        whole_block if fits else on_device,
         mesh=mesh,
         in_specs=placed,
         out_specs=P(("groups", "person"), "frame", None),

time: 271 us -> 99.8 us (0.37)
  Pallas kernels: 0 us -> 89.3 us
  waiting for transfers between devices: 81.7 us -> 0 us
  local copies, waits for them, and re-layouts: 80 us -> 8.73 us
  starting transfers between devices: 44.3 us -> 0 us
  matrix products: 29.4 us -> 0 us
  between operations: 14 us -> 0.02 us
  blocking collectives: 11.4 us -> 0 us
  other arithmetic: 8.98 us -> 1.35 us
    pallas_call x0 -> x1, Pallas kernels: none -> 89.3 us  [whole_block(): pl.pallas_call(block_kernel, out_shape=jax.ShapeDtypeStruct(tokens.shape,...]
    all_to_all x9 -> x0, waiting for transfers between devices: 80.3 us -> none  [the longest x1 26.6 us: on_device(): lax.all_to_all(queries, 'frame', split_axis=2, concat_axis=1, tiled=True)]
    all_to_all x9 -> x0, starting transfers between devices: 44.3 us -> none  [the longest x1 7.09 us: on_device(): lax.all_to_all(results, 'frame', split_axis=1, concat_axis=2, tiled=True)]
    unnamed x52 -> x17, local copies, waits for them, and re-layouts: 38.9 us -> 8.56 us
    dot_general x14 -> x0, matrix products: 29.4 us -> none  [the longest x2 12.6 us: project(): jnp.dot(flat_rows, weight, preferred_element_type=jnp.float32)]
    all_to_all x16 -> x0, local copies, waits for them, and re-layouts: 20.7 us -> none  [the longest x2 4.63 us: on_device(): lax.all_to_all(key_rows, 'frame', split_axis=2, concat_axis=1, tiled=True)]
    dot_general x4 -> x0, local copies, waits for them, and re-layouts: 13.9 us -> none  [the longest x1 8.65 us: project(): jnp.dot(flat_rows, weight, preferred_element_type=jnp.float32)]
    all_to_all x1 -> x0, blocking collectives: 11.4 us -> none  [on_device(): lax.all_to_all(results, 'person', split_axis=0, concat_axis=2, tiled=True)]
  transfers between devices with their start and end apart: 11 -> 0, of which waited for: 7 -> 0; matrix products, arithmetic and copies ran while one was open for 39% -> 0% of each run, Pallas kernels for 0% -> 0%
where the time goes in v1:
time: 99.8 us; the launch traced here: 99.4 us
  Pallas kernels  89.3 us (89%)
  local copies, waits for them, and re-layouts  8.73 us (9%)
  other arithmetic  1.35 us (1%)
    pallas_call x1, Pallas kernels, whole_block(): pl.pallas_call(block_kernel, out_shape=jax.ShapeDtypeStruct(tokens.shape,...  89.3 us
    unnamed x17, local copies, waits for them, and re-layouts  8.56 us

profile of v1, /device:TPU:0, one launch (start us, length us, event | category | flops | bytes accessed | tf_op | source)
XLA Modules:
  0.0 99.4 jit_solution(12595694288797576492)
XLA Ops:
  0.0 0.7 multiply_multiply_fusion.1
  0.7 0.7 multiply_multiply_fusion
  1.4 0.1 broadcast_in_dim_tile.7.gain_cross
  1.4 0.1 broadcast_in_dim_tile.6.gain_time
  1.5 0.0 copy-start
  1.5 1.6 %copy-done = bf16[1024,1024]{1,0:T(8,128)(2,1)S(1)} copy-done((bf16[1024,1024]{1,0:T(8,128)(2,1)S(1)}, bf16[1024,1024]{1,0:T(8,128)(2,1)}, u32[]{:S(2)}) %copy-start) | copy-done | bytes 2097176
  3.1 0.0 copy-start.1
  3.1 1.4 %copy-done.1 = bf16[256,3072]{1,0:T(8,128)(2,1)S(1)} copy-done((bf16[256,3072]{1,0:T(8,128)(2,1)S(1)}, bf16[256,3072]{1,0:T(8,128)(2,1)}, u32[]{:S(2)}) %copy-start.1) | copy-done | bytes 1572888
  4.5 0.0 copy-start.2
  4.5 1.0 %copy-done.2 = bf16[4,64,1024]{2,1,0:T(8,128)(2,1)S(1)} copy-done((bf16[4,64,1024]{2,1,0:T(8,128)(2,1)S(1)}, bf16[4,64,1024]{2,1,0:T(8,128)(2,1)}, u32[]{:S(2)}) %copy-start.2) | copy-done | bytes 524312
  5.6 0.0 copy-start.3
  5.6 1.0 %copy-done.3 = bf16[256,1024]{1,0:T(8,128)(2,1)S(1)} copy-done((bf16[256,1024]{1,0:T(8,128)(2,1)S(1)}, bf16[256,1024]{1,0:T(8,128)(2,1)}, u32[]{:S(2)}) %copy-start.3) | copy-done | bytes 524312
  6.6 0.0 copy-start.4
  6.6 0.7 copy-done.4
  7.3 0.0 copy-start.5
  7.3 0.7 copy-done.5
  8.0 0.0 copy-start.6
  8.0 0.7 copy-done.6
  8.6 0.0 copy-start.7
  8.6 0.7 copy-done.7
  9.3 89.3 %shard_map.127 = bf16[4,64,1024]{2,1,0:T(8,128)(2,1)S(1)} custom-call(s32[16]{0:T(128)S(1)} %copy-done.6, s32[16]{0:T(128)S(1)} %copy-done.7, bf16[4,64,1024]{2,1,0:T(8,128)(2,1)S(1)} %copy-done.2, f32[1,1024]{1,0:T(1,128)S(1)} %bitcast.2, bf16[1024,3072]{1,0:T(8,128)(2,1)} %qkv_time.1, f32[1,256]{1,0:T(1,128)S(1)} %broadcast_in_dim_tile.6.gain_time, ...), custom_call_target="tpu_custom_call" | custom-call | tf_op jit(solution)/shard_map/pallas_call | solution.py:356
  98.6 0.8 copy.15
  (2 shorter events, 0.0 us)
Async XLA Ops:
  1.5 1.6 %copy-start = (bf16[1024,1024]{1,0:T(8,128)(2,1)S(1)}, bf16[1024,1024]{1,0:T(8,128)(2,1)}, u32[]{:S(2)}) copy-start(bf16[1024,1024]{1,0:T(8,128)(2,1)} %out_time.1) | copy-start | bytes 6291460
  3.1 1.4 %copy-start.1 = (bf16[256,3072]{1,0:T(8,128)(2,1)S(1)}, bf16[256,3072]{1,0:T(8,128)(2,1)}, u32[]{:S(2)}) copy-start(bf16[256,3072]{1,0:T(8,128)(2,1)} %qkv_cross.1) | copy-start | bytes 4718596
  4.5 1.0 %copy-start.2 = (bf16[4,64,1024]{2,1,0:T(8,128)(2,1)S(1)}, bf16[4,64,1024]{2,1,0:T(8,128)(2,1)}, u32[]{:S(2)}) copy-start(bf16[4,64,1024]{2,1,0:T(8,128)(2,1)} %tokens.1) | copy-start | bytes 1572868
  5.6 1.0 %copy-start.3 = (bf16[256,1024]{1,0:T(8,128)(2,1)S(1)}, bf16[256,1024]{1,0:T(8,128)(2,1)}, u32[]{:S(2)}) copy-start(bf16[256,1024]{1,0:T(8,128)(2,1)} %out_cross.1) | copy-start | bytes 1572868
  6.6 0.7 copy-start.4
  7.3 0.7 copy-start.5
  8.0 0.7 copy-start.6
  8.6 0.7 copy-start.7

commit v2 on v1

--- a/solution.py
+++ b/solution.py
@@ -16,18 +16,28 @@
 
 
 def block_kernel(
+    tokens,
+    qkv_time,
+    out_time,
+    qkv_cross,
+    out_cross,
+    counts_in,
+    present_in,
+    norm_time_in,
+    norm_cross_in,
+    qgain_time_in,
+    kgain_time_in,
+    qgain_cross_in,
+    kgain_cross_in,
+    out,
     counts,
     present,
-    tokens,
     norm_time,
-    qkv_time,
-    gain_time,
-    out_time,
     norm_cross,
-    qkv_cross,
-    gain_cross,
-    out_cross,
-    out,
+    qgain_time,
+    kgain_time,
+    qgain_cross,
+    kgain_cross,
     tok,
     w_time,
     wo_time,
@@ -39,6 +49,7 @@
     mid_in,
     res,
     local_sem,
+    small_sem,
     tok_send,
     tok_recv,
     z_send,
@@ -93,7 +104,22 @@
             out_cross, w_cross.at[pl.ds(own, depth), pl.ds(3 * width, width)], local_sem.at[4]
         ),
     ]
-    for copy in local:
+    small = [
+        pltpu.make_async_copy(source, target, small_sem.at[k])
+        for k, (source, target) in enumerate(
+            (
+                (counts_in, counts),
+                (present_in, present),
+                (norm_time_in, norm_time),
+                (norm_cross_in, norm_cross),
+                (qgain_time_in, qgain_time),
+                (kgain_time_in, kgain_time),
+                (qgain_cross_in, qgain_cross),
+                (kgain_cross_in, kgain_cross),
+            )
+        )
+    ]
+    for copy in small + local:
         copy.start()
     pl.semaphore_wait(barrier, nx * nz)
 
@@ -185,8 +211,10 @@
         scale = lax.rsqrt(jnp.mean(stream * stream, axis=-1, keepdims=True) + 1e-06)
         return (stream * scale * gains).astype(BF16)
 
-    def attend(weight, gain):
+    def attend(weight, qgain, kgain, after):
         hidden = hid[...]
+        once = qgain[...] * kgain[...] * (3.0 / math.sqrt(HD))
+        gain = jnp.concatenate([once] * 4, axis=1)
 
         def project(column):
             return jnp.dot(hidden, weight[:, pl.ds(column, 256)], preferred_element_type=F32)
@@ -195,9 +223,9 @@
             squares = jnp.dot((entries * entries).astype(BF16), blocks, preferred_element_type=F32)
             return entries * lax.rsqrt(squares * (1.0 / HD) + 1e-06)
 
-        def step(t, carry):
-            column = pl.multiple_of(t * 256, 256)
-            queries = unit(project(column)) * gain[...]
+        for t in range(width // 256):
+            column = t * 256
+            queries = unit(project(column)) * gain
             keys = unit(project(width + column)).astype(BF16)
             values = project(2 * width + column).astype(BF16)
             for pair in range(2):
@@ -215,18 +243,24 @@
                 summed = jnp.where(low, sums[0][:, :128], sums[1][:, :128])
                 total = jnp.where(low, sums[0][:, 128:], sums[1][:, 128:])
                 att[:, pl.ds(column + pair * 128, 128)] = (summed / total).astype(BF16)
-            return carry
-
-        lax.fori_loop(0, width // 256, step, 0)
+            after(t)
 
     person = xc * nz + z
+    for copy in small:
+        copy.wait()
     bias[...] = jnp.where(key_index < counts[person], 0.0, -1e30)
     local[0].wait()
     for d in (1, 3, 2):
         tok_copy(zs(d), zs(d), d, zs(d)).wait_recv()
     hid[...] = normed(tok[...].reshape(rows, width).astype(F32), norm_time[...])
     local[1].wait()
-    attend(w_time, gain_time)
+    early = {0: 1, 1: 3, 2: 2}
+
+    def spread(t):
+        if t in early:
+            forward(0, early[t])
+
+    attend(w_time, qgain_time, kgain_time, spread)
     local[2].wait()
 
     def temporal_out(t, carry):
@@ -258,7 +292,7 @@
     mid_in[pl.ds(into, part), :] = mid[pl.ds(start, part), :]
 
     for d in (1, 3, 2):
-        forward(0, d)
+        forward(1, d)
 
     key_row = lax.broadcasted_iota(jnp.int32, (8, rows), 1)
     limit = jnp.zeros((8, rows), jnp.int32)
@@ -271,19 +305,17 @@
     bias[...] = jnp.where(allowed, 0.0, -1e30)
 
     for d in (1, 3, 2):
-        forward(1, d)
+        forward(2, d)
     for i, d in offsets:
         source = xs(i) * nz + zs(d)
         mid_copy(i, d, xc, z, source, {"person": xs(i), "frame": zs(d)}).wait_recv()
     hid[...] = normed(mid_in[...].astype(F32), norm_cross[...])
-    for d in (1, 3, 2):
-        forward(2, d)
     local[3].wait()
     local[4].wait()
     for d in (1, 3, 2):
         for half in range(2):
             hop_copy(2, half, d, True).wait_recv()
-    attend(w_cross, gain_cross)
+    attend(w_cross, qgain_cross, kgain_cross, lambda t: None)
 
     def cross_out(t, carry):
         column = pl.multiple_of(t * 256, 256)
@@ -346,31 +378,22 @@
 ):
     persons, frames, width = tokens.shape
     rows = persons * frames
-    scale = 3.0 / math.sqrt(HD)
-    gain_time = jnp.tile(qgain_time * kgain_time * scale, 4)[None, :]
-    gain_cross = jnp.tile(qgain_cross * kgain_cross * scale, 4)[None, :]
-    smem = pl.BlockSpec(memory_space=pltpu.SMEM)
-    vmem = pl.BlockSpec(memory_space=pltpu.VMEM)
     anywhere = pl.BlockSpec(memory_space=pl.ANY)
     dma = pltpu.SemaphoreType.DMA
     return pl.pallas_call(
         block_kernel,
         out_shape=jax.ShapeDtypeStruct(tokens.shape, BF16),
-        in_specs=[
-            smem,
-            smem,
-            anywhere,
-            vmem,
-            anywhere,
-            vmem,
-            anywhere,
-            vmem,
-            anywhere,
-            vmem,
-            anywhere,
-        ],
+        in_specs=[anywhere] * 13,
         out_specs=anywhere,
         scratch_shapes=[
+            pltpu.SMEM(frame_counts.shape, jnp.int32),
+            pltpu.SMEM(presence.shape, jnp.int32),
+            pltpu.VMEM((1, width), F32),
+            pltpu.VMEM((1, width), F32),
+            pltpu.VMEM((1, HD), F32),
+            pltpu.VMEM((1, HD), F32),
+            pltpu.VMEM((1, HD), F32),
+            pltpu.VMEM((1, HD), F32),
             pltpu.VMEM(tokens.shape, BF16),
             pltpu.VMEM((width, 3 * width), BF16),
             pltpu.VMEM((width, width), BF16),
@@ -382,6 +405,7 @@
             pltpu.VMEM((rows, width), BF16),
             pltpu.VMEM((16, rows // 16, width), BF16),
             dma((6,)),
+            dma((8,)),
             dma((3,)),
             dma((3,)),
             dma((2, 3, 2)),
@@ -394,20 +418,22 @@
             dma((3,)),
         ],
         compiler_params=pltpu.CompilerParams(
-            collective_id=0, has_side_effects=True, vmem_limit_bytes=48 * 1024 * 1024
+            collective_id=0, has_side_effects=True, vmem_limit_bytes=60 * 1024 * 1024
         ),
     )(
+        tokens,
+        qkv_time,
+        out_time,
+        qkv_cross,
+        out_cross,
         frame_counts,
         presence,
-        tokens,
         norm_time[None, :],
-        qkv_time,
-        gain_time,
-        out_time,
         norm_cross[None, :],
-        qkv_cross,
-        gain_cross,
-        out_cross,
+        qgain_time[None, :],
+        kgain_time[None, :],
+        qgain_cross[None, :],
+        kgain_cross[None, :],
     )
 
 

time: 99.8 us -> 88.5 us (0.89)
  local copies, waits for them, and re-layouts: 8.73 us -> 1.87 us
  Pallas kernels: 89.3 us -> 86.4 us
  other arithmetic: 1.35 us -> 0 us
    unnamed x17 -> x1, local copies, waits for them, and re-layouts: 8.56 us -> 1.87 us
    pallas_call x1, Pallas kernels: 89.3 us -> 86.4 us  [whole_block(): pl.pallas_call(block_kernel, out_shape=jax.ShapeDtypeStruct(tokens.shape,...]
    mul x2 -> x0, other arithmetic: 1.35 us -> none  [the longest x1 0.67 us: whole_block(): gain_time = jnp.tile(qgain_time * kgain_time * scale, 4)[None, :]]
where the time goes in v2:
time: 88.5 us; the launch traced here: 88.3 us
  Pallas kernels  86.4 us (98%)
  local copies, waits for them, and re-layouts  1.87 us (2%)
    pallas_call x1, Pallas kernels, whole_block(): pl.pallas_call(block_kernel, out_shape=jax.ShapeDtypeStruct(tokens.shape,...  86.4 us
    unnamed x1, local copies, waits for them, and re-layouts  1.87 us

profile of v2, /device:TPU:0, one launch (start us, length us, event | category | flops | bytes accessed | tf_op | source)
XLA Modules:
  0.0 88.3 jit_solution(5094793593723133334)
XLA Ops:
  0.0 86.4 %shard_map.127 = bf16[4,64,1024]{2,1,0:T(8,128)(2,1)} custom-call(bf16[4,64,1024]{2,1,0:T(8,128)(2,1)} %tokens.1, bf16[1024,3072]{1,0:T(8,128)(2,1)} %qkv_time.1, bf16[1024,1024]{1,0:T(8,128)(2,1)} %out_time.1, bf16[256,3072]{1,0:T(8,128)(2,1)} %qkv_cross.1, bf16[256,1024]{1,0:T(8,128)(2,1)} %out_cross.1, s32[16]{0:T(128)} %counts_in.1, s32[16]{0:T(128)} %present_in.1, ...), custom_call_target="tpu_custom_call" | custom-call | tf_op jit(solution)/shard_map/pallas_call | solution.py:383
  86.4 1.9 %copy.15 = bf16[4,64,1024]{2,1,0:T(8,128)(2,1)} copy(bf16[4,64,1024]{2,1,0:T(8,128)(2,1)} %shard_map.127) | data formatting | bytes 1048576

commit v3 on v2

--- a/solution.py
+++ b/solution.py
@@ -140,24 +140,41 @@
         slot = core * 4 + (group * 2 + x if half == 0 else x * 2 + group)
         return half * (depth // 2) + slot * piece
 
-    def z_copy(half, d, array, source, peer):
-        start = pl.multiple_of(at_piece(half), piece)
-        into = pl.multiple_of(source * depth + at_piece(half), piece)
-        ref = (qkv_cross, out_cross)[array]
-        columns = (pl.ds(0, 3 * width), pl.ds(3 * width, width))[array]
+    def z_copy(half, d, way, shard, peer):
+        start = pl.multiple_of(shard * depth + at_piece(half), piece)
+        block = w_cross.at[pl.ds(start, piece), :]
         return pltpu.make_async_remote_copy(
-            src_ref=ref.at[pl.ds(start, piece), :],
-            dst_ref=w_cross.at[pl.ds(into, piece), columns],
-            send_sem=z_send.at[half, d - 1, array],
-            recv_sem=z_recv.at[half, d - 1, array],
+            src_ref=block,
+            dst_ref=block,
+            send_sem=z_send.at[half, d - 1, way],
+            recv_sem=z_recv.at[half, d - 1],
             device_id={"frame": peer},
             device_id_type=MESH,
         )
 
-    for d in (1, 3, 2):
-        for half in range(2):
-            for array in range(2):
-                z_copy(half, d, array, z, zt(d)).start()
+    def pass_on(k, act):
+        @pl.when((z + 1 < nz) & (z >= k - 1))
+        def _():
+            for half in range(2):
+                act(z_copy(half, k, 0, zs(k - 1), zt(1)))
+
+        @pl.when((z >= 1) & (z + k - 1 < nz))
+        def _():
+            for half in range(2):
+                act(z_copy(half, nz - k, 1, zt(k - 1), zs(1)))
+
+    def by_arrival(k, act):
+        @pl.when(z >= k)
+        def _():
+            act(k)
+
+        @pl.when(z + k < nz)
+        def _():
+            act(nz - k)
+
+    local[3].wait()
+    local[4].wait()
+    pass_on(1, lambda copy: copy.start())
 
     def hop_copy(hop, half, d, incoming):
         along_x = (half == 0) == (hop == 0)
@@ -189,12 +206,16 @@
     def forward(hop, d):
         for half in range(2):
             if hop == 0:
-                for array in range(2):
-                    z_copy(half, d, array, zs(d), zs(d)).wait_recv()
+                z_copy(half, d, 0, zs(d), zs(1)).wait_recv()
             else:
                 hop_copy(hop - 1, half, d, True).wait_recv()
         for half in range(2):
             hop_copy(hop, half, d, False).start()
+
+    def arrive(k):
+        by_arrival(k, functools.partial(forward, 0))
+        if k + 1 < nz:
+            pass_on(k + 1, lambda copy: copy.start())
 
     lane = lax.broadcasted_iota(jnp.int32, (rows, 128), 1)
     low = lane < HD
@@ -249,16 +270,19 @@
     for copy in small:
         copy.wait()
     bias[...] = jnp.where(key_index < counts[person], 0.0, -1e30)
+    arrive(1)
     local[0].wait()
     for d in (1, 3, 2):
         tok_copy(zs(d), zs(d), d, zs(d)).wait_recv()
     hid[...] = normed(tok[...].reshape(rows, width).astype(F32), norm_time[...])
     local[1].wait()
-    early = {0: 1, 1: 3, 2: 2}
-
     def spread(t):
-        if t in early:
-            forward(0, early[t])
+        if t == 0:
+            arrive(2)
+        if t == 2:
+            arrive(3)
+        if t == 3:
+            by_arrival(1, functools.partial(forward, 1))
 
     attend(w_time, qgain_time, kgain_time, spread)
     local[2].wait()
@@ -291,8 +315,8 @@
     start = pl.multiple_of(z * frames + xc * part, part)
     mid_in[pl.ds(into, part), :] = mid[pl.ds(start, part), :]
 
-    for d in (1, 3, 2):
-        forward(1, d)
+    for k in (2, 3):
+        by_arrival(k, functools.partial(forward, 1))
 
     key_row = lax.broadcasted_iota(jnp.int32, (8, rows), 1)
     limit = jnp.zeros((8, rows), jnp.int32)
@@ -304,14 +328,12 @@
     allowed = ((key_index % part == query_index % part) & (usable > 0)) | (key_index == query_index)
     bias[...] = jnp.where(allowed, 0.0, -1e30)
 
-    for d in (1, 3, 2):
-        forward(2, d)
+    for k in (1, 2, 3):
+        by_arrival(k, functools.partial(forward, 2))
     for i, d in offsets:
         source = xs(i) * nz + zs(d)
         mid_copy(i, d, xc, z, source, {"person": xs(i), "frame": zs(d)}).wait_recv()
     hid[...] = normed(mid_in[...].astype(F32), norm_cross[...])
-    local[3].wait()
-    local[4].wait()
     for d in (1, 3, 2):
         for half in range(2):
             hop_copy(2, half, d, True).wait_recv()
@@ -349,10 +371,9 @@
     for d in (1, 2, 3):
         tok_copy(zt(d), z, d, zt(d)).wait_send()
         for half in range(2):
-            for array in range(2):
-                z_copy(half, d, array, z, zt(d)).wait_send()
             for hop in range(3):
                 hop_copy(hop, half, d, False).wait_send()
+        pass_on(d, lambda copy: copy.wait_send())
     for i, d in offsets:
         mid_copy(i, d, xt(i), zt(d), person, {"person": xt(i), "frame": zt(d)}).wait_send()
     kept.wait()
@@ -409,7 +430,7 @@
             dma((3,)),
             dma((3,)),
             dma((2, 3, 2)),
-            dma((2, 3, 2)),
+            dma((2, 3)),
             dma((3, 2, 3)),
             dma((3, 2, 3)),
             dma((4, 4)),

time: 88.5 us -> 82.8 us (0.936)
  Pallas kernels: 86.4 us -> 80.8 us
    pallas_call x1, Pallas kernels: 86.4 us -> 80.8 us  [whole_block(): pl.pallas_call(block_kernel, out_shape=jax.ShapeDtypeStruct(tokens.shape,...]
where the time goes in v3:
time: 82.8 us; the launch traced here: 82.7 us
  Pallas kernels  80.8 us (98%)
  local copies, waits for them, and re-layouts  1.87 us (2%)
    pallas_call x1, Pallas kernels, whole_block(): pl.pallas_call(block_kernel, out_shape=jax.ShapeDtypeStruct(tokens.shape,...  80.8 us
    unnamed x1, local copies, waits for them, and re-layouts  1.87 us

profile of v3, /device:TPU:0, one launch (start us, length us, event | category | flops | bytes accessed | tf_op | source)
XLA Modules:
  0.0 82.7 jit_solution(10148452327787485589)
XLA Ops:
  0.0 80.8 %shard_map.127 = bf16[4,64,1024]{2,1,0:T(8,128)(2,1)} custom-call(bf16[4,64,1024]{2,1,0:T(8,128)(2,1)} %tokens.1, bf16[1024,3072]{1,0:T(8,128)(2,1)} %qkv_time.1, bf16[1024,1024]{1,0:T(8,128)(2,1)} %out_time.1, bf16[256,3072]{1,0:T(8,128)(2,1)} %qkv_cross.1, bf16[256,1024]{1,0:T(8,128)(2,1)} %out_cross.1, s32[16]{0:T(128)} %counts_in.1, s32[16]{0:T(128)} %present_in.1, ...), custom_call_target="tpu_custom_call" | custom-call | tf_op jit(solution)/shard_map/pallas_call | solution.py:404
  80.8 1.9 %copy.15 = bf16[4,64,1024]{2,1,0:T(8,128)(2,1)} copy(bf16[4,64,1024]{2,1,0:T(8,128)(2,1)} %shard_map.127) | data formatting | bytes 1048576

commit v4 on v3

--- a/solution.py
+++ b/solution.py
@@ -119,7 +119,7 @@
             )
         )
     ]
-    for copy in small + local:
+    for copy in local[3:] + local[:3] + small:
         copy.start()
     pl.semaphore_wait(barrier, nx * nz)
 
@@ -132,9 +132,6 @@
             device_id={"frame": peer},
             device_id_type=MESH,
         )
-
-    for d in (2, 1, 3):
-        tok_copy(zt(d), z, d, zt(d)).start()
 
     def at_piece(half):
         slot = core * 4 + (group * 2 + x if half == 0 else x * 2 + group)
@@ -175,8 +172,10 @@
     local[3].wait()
     local[4].wait()
     pass_on(1, lambda copy: copy.start())
-
-    def hop_copy(hop, half, d, incoming):
+    for d in (2, 1, 3):
+        tok_copy(zt(d), z, d, zt(d)).start()
+
+    def hop_copy(hop, half, d, incoming, columns=None):
         along_x = (half == 0) == (hop == 0)
         if hop == 2:
             side = 1 - core if incoming else core
@@ -193,12 +192,14 @@
         start = pl.multiple_of(
             zs(d) * depth + half * (depth // 2) + offset * piece, length * piece
         )
-        block = w_cross.at[pl.ds(start, length * piece), :]
+        first, count = ((0, 4), (0, 3), (3, 1))[0 if columns is None else columns + 1]
+        block = w_cross.at[pl.ds(start, length * piece), pl.ds(first * width, count * width)]
+        slot = hop if columns is None else hop + columns
         return pltpu.make_async_remote_copy(
             src_ref=block,
             dst_ref=block,
-            send_sem=hop_send.at[hop, half, d - 1],
-            recv_sem=hop_recv.at[hop, half, d - 1],
+            send_sem=hop_send.at[slot, half, d - 1],
+            recv_sem=hop_recv.at[slot, half, d - 1],
             device_id=device,
             device_id_type=MESH,
         )
@@ -210,7 +211,7 @@
             else:
                 hop_copy(hop - 1, half, d, True).wait_recv()
         for half in range(2):
-            hop_copy(hop, half, d, False).start()
+            hop_copy(hop, half, d, False, 0 if hop == 2 else None).start()
 
     def arrive(k):
         by_arrival(k, functools.partial(forward, 0))
@@ -275,14 +276,14 @@
     for d in (1, 3, 2):
         tok_copy(zs(d), zs(d), d, zs(d)).wait_recv()
     hid[...] = normed(tok[...].reshape(rows, width).astype(F32), norm_time[...])
+    arrive(2)
     local[1].wait()
     def spread(t):
-        if t == 0:
-            arrive(2)
-        if t == 2:
+        if t == 1:
+            by_arrival(1, functools.partial(forward, 1))
             arrive(3)
         if t == 3:
-            by_arrival(1, functools.partial(forward, 1))
+            by_arrival(2, functools.partial(forward, 1))
 
     attend(w_time, qgain_time, kgain_time, spread)
     local[2].wait()
@@ -315,8 +316,7 @@
     start = pl.multiple_of(z * frames + xc * part, part)
     mid_in[pl.ds(into, part), :] = mid[pl.ds(start, part), :]
 
-    for k in (2, 3):
-        by_arrival(k, functools.partial(forward, 1))
+    by_arrival(3, functools.partial(forward, 1))
 
     key_row = lax.broadcasted_iota(jnp.int32, (8, rows), 1)
     limit = jnp.zeros((8, rows), jnp.int32)
@@ -330,14 +330,21 @@
 
     for k in (1, 2, 3):
         by_arrival(k, functools.partial(forward, 2))
+    for d in (1, 2, 3):
+        for half in range(2):
+            hop_copy(2, half, d, False, 1).start()
     for i, d in offsets:
         source = xs(i) * nz + zs(d)
         mid_copy(i, d, xc, z, source, {"person": xs(i), "frame": zs(d)}).wait_recv()
     hid[...] = normed(mid_in[...].astype(F32), norm_cross[...])
     for d in (1, 3, 2):
         for half in range(2):
-            hop_copy(2, half, d, True).wait_recv()
+            hop_copy(2, half, d, True, 0).wait_recv()
     attend(w_cross, qgain_cross, kgain_cross, lambda t: None)
+
+    for d in (1, 2, 3):
+        for half in range(2):
+            hop_copy(2, half, d, True, 1).wait_recv()
 
     def cross_out(t, carry):
         column = pl.multiple_of(t * 256, 256)
@@ -371,8 +378,10 @@
     for d in (1, 2, 3):
         tok_copy(zt(d), z, d, zt(d)).wait_send()
         for half in range(2):
-            for hop in range(3):
+            for hop in range(2):
                 hop_copy(hop, half, d, False).wait_send()
+            for columns in range(2):
+                hop_copy(2, half, d, False, columns).wait_send()
         pass_on(d, lambda copy: copy.wait_send())
     for i, d in offsets:
         mid_copy(i, d, xt(i), zt(d), person, {"person": xt(i), "frame": zt(d)}).wait_send()
@@ -431,8 +440,8 @@
             dma((3,)),
             dma((2, 3, 2)),
             dma((2, 3)),
-            dma((3, 2, 3)),
-            dma((3, 2, 3)),
+            dma((4, 2, 3)),
+            dma((4, 2, 3)),
             dma((4, 4)),
             dma((4, 4)),
             dma((3,)),

time: 82.8 us -> 76.8 us (0.928)
  Pallas kernels: 80.8 us -> 74.7 us
    pallas_call x1, Pallas kernels: 80.8 us -> 74.7 us  [whole_block(): pl.pallas_call(block_kernel, out_shape=jax.ShapeDtypeStruct(tokens.shape,...]
where the time goes in v4:
time: 76.8 us; the launch traced here: 76.6 us
  Pallas kernels  74.7 us (97%)
  local copies, waits for them, and re-layouts  1.87 us (2%)
    pallas_call x1, Pallas kernels, whole_block(): pl.pallas_call(block_kernel, out_shape=jax.ShapeDtypeStruct(tokens.shape,...  74.7 us
    unnamed x1, local copies, waits for them, and re-layouts  1.87 us

profile of v4, /device:TPU:0, one launch (start us, length us, event | category | flops | bytes accessed | tf_op | source)
XLA Modules:
  0.0 76.6 jit_solution(7530581542702138021)
XLA Ops:
  0.0 74.7 %shard_map.127 = bf16[4,64,1024]{2,1,0:T(8,128)(2,1)} custom-call(bf16[4,64,1024]{2,1,0:T(8,128)(2,1)} %tokens.1, bf16[1024,3072]{1,0:T(8,128)(2,1)} %qkv_time.1, bf16[1024,1024]{1,0:T(8,128)(2,1)} %out_time.1, bf16[256,3072]{1,0:T(8,128)(2,1)} %qkv_cross.1, bf16[256,1024]{1,0:T(8,128)(2,1)} %out_cross.1, s32[16]{0:T(128)} %counts_in.1, s32[16]{0:T(128)} %present_in.1, ...), custom_call_target="tpu_custom_call" | custom-call | tf_op jit(solution)/shard_map/pallas_call | solution.py:413
  74.8 1.9 %copy.15 = bf16[4,64,1024]{2,1,0:T(8,128)(2,1)} copy(bf16[4,64,1024]{2,1,0:T(8,128)(2,1)} %shard_map.127) | data formatting | bytes 1048576
